TPU v7x, 32 devices: a whole 2x2x4 slice. The times are simulated.
32 devices in a mesh: dp: 4 (over y, x), segment: 4 (over z), chan: 2 (over core).
Axes of the slice: x: 2, y: 2, z: 4, core: 2. Of those that a mesh axis runs over, the one named last changes fastest.
Arguments:
- x_input: bfloat16 [4, 4, 256, 1024], P(None, 'dp', None, 'chan'), may hold values from -48 to 48
- d_output: bfloat16 [4, 4, 256, 1024], P(None, 'dp', None, 'chan'), may hold values from -6 to 6
- weights: bfloat16 [4, 9, 1024, 1024], P('segment', None, None, 'chan'), may hold values from -0.0625 to 0.0625
- gains: float32 [4, 1024], P('segment', 'chan'), may hold values from 0.5 to 1.5
- biases: float32 [4, 1024], P('segment', 'chan'), may hold values from -3 to 3
Outputs:
- d_weights: float32 [4, 9, 1024, 1024], P('segment', None, None, 'chan')
- d_gains: float32 [4, 1024], P('segment', 'chan')
- d_biases: float32 [4, 1024], P('segment', 'chan')
All inputs are finite; a program needn't handle non-finite values.
Results may differ from a plain program's by a relative error of at most 0.025.
Values may be sent and summed in bfloat16 or wider, within the bound.
A program may use at most 128 MiB of HBM per device.

v0:
```python
import jax
import jax.numpy as jnp
from jax import lax
from jax.sharding import PartitionSpec as P

GROUPS = 32
SIDE = 16


EPSILON = 1e-05


def shifted(shard, axis, by):
    length = lax.axis_size(axis)
    pairs = [(i, i + by) for i in range(length) if 0 <= i + by < length]
    return lax.ppermute(shard, axis, pairs)


def expand_groups(statistic, group_width):
    return jnp.repeat(statistic, group_width, axis=1)[:, None, :]


def group_sums(values, group_width):
    batch_count, pixel_count, channels = values.shape
    grouped = values.reshape(batch_count, pixel_count, channels // group_width, group_width)
    return jnp.sum(grouped, axis=(1, 3))


def shifted_stack(images, forward_taps):
    batch_count, pixel_count, channels = images.shape
    square = images.reshape(batch_count, SIDE, SIDE, channels)
    padded = jnp.pad(square, ((0, 0), (1, 1), (1, 1), (0, 0)))
    tap_list = []
    for tap_y in range(3):
        for tap_x in range(3):
            start_y = tap_y if forward_taps else 2 - tap_y
            start_x = tap_x if forward_taps else 2 - tap_x
            window = padded[:, start_y : start_y + SIDE, start_x : start_x + SIDE, :]
            tap_list.append(window.reshape(batch_count * pixel_count, channels))
    return jnp.stack(tap_list)


def take_slot(buffer, slot_index):
    return lax.dynamic_index_in_dim(buffer, slot_index, 0, keepdims=False)


def put_slot(buffer, value, slot_index, allowed):
    current = take_slot(buffer, slot_index)
    return lax.dynamic_update_index_in_dim(
        buffer, jnp.where(allowed, value, current), slot_index, 0
    )


def local(x_input, d_output, weights, gains, biases):
    segments = lax.axis_size("segment")
    half_way = segments // 2
    position = lax.axis_index("segment")
    is_down = position < half_way
    level = jnp.where(is_down, position, 2 * half_way - 1 - position)
    weight = weights[0]
    gain_row = gains[0]
    bias_row = biases[0]
    micro_count, images, pixels, local_width = x_input.shape
    full_width = weight.shape[1]
    group_width = full_width // GROUPS
    local_groups = local_width // group_width
    row_count = images * pixels
    group_count = pixels * group_width
    tick_count = micro_count + segments - 1
    bwd_place = 2 * half_way - 1 - position
    act_shape = (images, pixels, local_width)
    below_slot = jnp.clip(position - 1, 0, half_way - 1)
    above_slot = jnp.clip(level + 1, 0, half_way - 1)
    has_above = level < half_way - 1
    before_slot = jnp.clip(level - 1, 0, half_way - 1)

    def normalize(values, group_mean, group_rstd):
        normed = (values - expand_groups(group_mean, group_width)) * expand_groups(
            group_rstd, group_width
        )
        return (normed, normed * gain_row + bias_row)

    def forward_tick(tick_index, loop_state):
        stack_recv, saved_inputs, saved_mean, saved_rstd, saved_full = loop_state
        micro_index = tick_index - position
        active = (micro_index >= 0) & (micro_index < micro_count)
        slot_index = jnp.clip(micro_index, 0, micro_count - 1)
        first_in = jnp.where(
            position == 0, take_slot(x_input, slot_index), take_slot(stack_recv, below_slot)
        )
        skip_part = take_slot(stack_recv, level).astype(jnp.float32)
        upper_part = jnp.where(
            has_above, take_slot(stack_recv, above_slot).astype(jnp.float32), 0.0
        )
        joined = (upper_part + skip_part).astype(jnp.bfloat16)
        inputs = jnp.where(is_down, first_in, joined)
        values = inputs.astype(jnp.float32)
        group_mean = group_sums(values, group_width) / group_count
        centred = values - expand_groups(group_mean, group_width)
        variance = group_sums(centred * centred, group_width) / group_count
        group_rstd = lax.rsqrt(variance + EPSILON)
        normed, pre_act = normalize(values, group_mean, group_rstd)
        hidden = (pre_act * jax.nn.sigmoid(pre_act)).astype(jnp.bfloat16)
        empty_sum = jnp.zeros((row_count, local_width), jnp.float32)
        shard_piece = lax.all_gather(hidden, "chan", axis=2, tiled=True)
        conv_out = lax.cond(
            active,
            lambda: empty_sum
            + jnp.einsum(
                "trc,tco->ro",
                shifted_stack(shard_piece, True),
                weight,
                preferred_element_type=jnp.float32,
            ),
            lambda: empty_sum,
        )
        output = (values + conv_out.reshape(act_shape)).astype(jnp.bfloat16)
        saved_inputs = put_slot(saved_inputs, inputs, slot_index, active)
        saved_mean = put_slot(saved_mean, group_mean, slot_index, active)
        saved_rstd = put_slot(saved_rstd, group_rstd, slot_index, active)
        outgoing = put_slot(stack_recv, output, level, True)
        next_stack = shifted(outgoing, "segment", 1)
        return (next_stack, saved_inputs, saved_mean, saved_rstd, saved_full)

    zero_stack = jnp.zeros((half_way,) + act_shape, jnp.bfloat16)
    zero_buffer = jnp.zeros((micro_count,) + act_shape, jnp.bfloat16)
    zero_stats = jnp.zeros((micro_count, images, local_groups), jnp.float32)
    full_init = jnp.zeros((1,), jnp.bfloat16)
    forward_state = lax.fori_loop(
        0, tick_count, forward_tick, (zero_stack, zero_buffer, zero_stats, zero_stats, full_init)
    )
    saved_inputs, saved_mean, saved_rstd, saved_full = (
        forward_state[1],
        forward_state[2],
        forward_state[3],
        forward_state[4],
    )

    def backward_tick(tick_index, loop_state):
        grad_stack, grad_weight, grad_gain, grad_bias = loop_state
        micro_index = tick_index - bwd_place
        active = (micro_index >= 0) & (micro_index < micro_count)
        slot_index = jnp.clip(micro_index, 0, micro_count - 1)
        own_part = take_slot(grad_stack, level).astype(jnp.float32)
        later_part = jnp.where(
            has_above, take_slot(grad_stack, above_slot).astype(jnp.float32), 0.0
        )
        down_grad = (own_part + later_part).astype(jnp.bfloat16)
        up_grad = jnp.where(
            level == 0, take_slot(d_output, slot_index), take_slot(grad_stack, before_slot)
        )
        grad_out = jnp.where(is_down, down_grad, up_grad)
        values = take_slot(saved_inputs, slot_index).astype(jnp.float32)
        group_mean = take_slot(saved_mean, slot_index)
        group_rstd = take_slot(saved_rstd, slot_index)
        normed, pre_act = normalize(values, group_mean, group_rstd)
        sigma = jax.nn.sigmoid(pre_act)
        grad_rows = grad_out.reshape(row_count, local_width)
        hidden = (pre_act * sigma).astype(jnp.bfloat16)
        shard_piece = lax.all_gather(hidden, "chan", axis=2, tiled=True)
        grad_weight = grad_weight + lax.cond(
            active,
            lambda: jnp.einsum(
                "trc,ro->tco",
                shifted_stack(shard_piece, True),
                grad_rows,
                preferred_element_type=jnp.float32,
            ),
            lambda: jnp.zeros((9, shard_piece.shape[2], local_width), jnp.float32),
        )
        partial_grad = lax.cond(
            active,
            lambda: jnp.einsum(
                "tro,tco->rc",
                shifted_stack(grad_out, False),
                weight,
                preferred_element_type=jnp.float32,
            ),
            lambda: jnp.zeros((row_count, full_width), jnp.float32),
        )
        grad_hidden = lax.psum_scatter(
            partial_grad.reshape(images, pixels, full_width).astype(jnp.bfloat16),
            "chan",
            scatter_dimension=2,
            tiled=True,
        ).astype(jnp.float32)
        grad_pre = grad_hidden * sigma * (1.0 + pre_act * (1.0 - sigma))
        grad_gain = grad_gain + jnp.where(active, jnp.sum(grad_pre * normed, axis=(0, 1)), 0.0)
        grad_bias = grad_bias + jnp.where(active, jnp.sum(grad_pre, axis=(0, 1)), 0.0)
        grad_normed = grad_pre * gain_row
        first_mean = expand_groups(group_sums(grad_normed, group_width) / group_count, group_width)
        second_mean = expand_groups(
            group_sums(grad_normed * normed, group_width) / group_count, group_width
        )
        grad_in = (
            grad_out.astype(jnp.float32)
            + expand_groups(group_rstd, group_width)
            * (grad_normed - first_mean - normed * second_mean)
        ).astype(jnp.bfloat16)
        outgoing = put_slot(grad_stack, grad_in, level, True)
        next_stack = shifted(outgoing, "segment", -1)
        return (next_stack, grad_weight, grad_gain, grad_bias)

    backward_init = (
        zero_stack,
        jnp.zeros(weight.shape, jnp.float32),
        jnp.zeros((local_width,), jnp.float32),
        jnp.zeros((local_width,), jnp.float32),
    )
    backward_state = lax.fori_loop(0, tick_count, backward_tick, backward_init)
    grad_weight, grad_gain, grad_bias = (
        lax.psum(backward_state[1].astype(jnp.bfloat16), "dp").astype(jnp.float32),
        lax.psum(backward_state[2].astype(jnp.bfloat16), "dp").astype(jnp.float32),
        lax.psum(backward_state[3].astype(jnp.bfloat16), "dp").astype(jnp.float32),
    )
    return (grad_weight[None], grad_gain[None], grad_bias[None])


def solution(mesh):
    in_specs = (
        P(None, "dp", None, "chan"),
        P(None, "dp", None, "chan"),
        P("segment", None, None, "chan"),
        P("segment", "chan"),
        P("segment", "chan"),
    )
    out_specs = (P("segment", None, None, "chan"), P("segment", "chan"), P("segment", "chan"))
    return jax.shard_map(local, mesh=mesh, in_specs=in_specs, out_specs=out_specs, check_vma=False)
```

profile of v0, /device:TPU:0, one launch (start us, length us, event | category | flops | bytes accessed | tf_op | source)
XLA Modules:
  0.0 932.3 jit_solution(9440757152164669471)
XLA Ops:
  8.2 184.8 %while.47 = (s32[]{:T(128)}, bf16[2,1,256,512]{3,2,1,0:T(8,128)(2,1)S(1)}, bf16[4,1,256,512]{3,2,1,0:T(8,128)(2,1)S(1)}, f32[4,1,16]{2,1,0:T(1,128)S(1)}, f32[4,...) while((s32[]{:T(128)}, ...), condition=%wide.region_7.8_spmd, body=%wide.region_0.7_spmd.sunk | while | flops 2419458048 | bytes 74491776 | solution.py:129
  21.8 11.9 %collective-permute-done = bf16[2,1,256,512]{3,2,1,0:T(8,128)(2,1)S(1)} collective-permute-done((bf16[2,1,256,512]{3,2,1,0:T(8,128)(2,1)S(1)}, bf16[2,1,256,512]{3,2,1,0:T(8,128)(2,1)S(1)}, u32[]{:S(2)}, u32[]{:S(2)}) %collective-permute-start) | collective-permute-done | bytes 524320 | tf_op jit(solution)/shard_map/while/body/eval_jaxpr/ppermute | solution.py:16
  50.4 11.4 %collective-permute-done = bf16[2,1,256,512]{3,2,1,0:T(8,128)(2,1)S(1)} collective-permute-done((bf16[2,1,256,512]{3,2,1,0:T(8,128)(2,1)S(1)}, bf16[2,1,256,512]{3,2,1,0:T(8,128)(2,1)S(1)}, u32[]{:S(2)}, u32[]{:S(2)}) %collective-permute-start) | collective-permute-done | bytes 524320 | tf_op jit(solution)/shard_map/while/body/eval_jaxpr/ppermute | solution.py:16
  78.4 11.4 %collective-permute-done = bf16[2,1,256,512]{3,2,1,0:T(8,128)(2,1)S(1)} collective-permute-done((bf16[2,1,256,512]{3,2,1,0:T(8,128)(2,1)S(1)}, bf16[2,1,256,512]{3,2,1,0:T(8,128)(2,1)S(1)}, u32[]{:S(2)}, u32[]{:S(2)}) %collective-permute-start) | collective-permute-done | bytes 524320 | tf_op jit(solution)/shard_map/while/body/eval_jaxpr/ppermute | solution.py:16
  106.5 11.4 %collective-permute-done = bf16[2,1,256,512]{3,2,1,0:T(8,128)(2,1)S(1)} collective-permute-done((bf16[2,1,256,512]{3,2,1,0:T(8,128)(2,1)S(1)}, bf16[2,1,256,512]{3,2,1,0:T(8,128)(2,1)S(1)}, u32[]{:S(2)}, u32[]{:S(2)}) %collective-permute-start) | collective-permute-done | bytes 524320 | tf_op jit(solution)/shard_map/while/body/eval_jaxpr/ppermute | solution.py:16
  193.9 519.5 %while.48 = (s32[]{:T(128)}, bf16[2,1,256,512]{3,2,1,0:T(8,128)(2,1)}, f32[9,1024,512]{2,1,0:T(8,128)}, f32[512]{0:T(512)S(1)}, f32[512]{0:T(512)S(1)}, /*index=...) while((s32[]{:T(128)}, ...), condition=%wide.region_20.21_spmd.clone, body=%wide.region_8.20_spmd.clone.sunk | while | flops 4846913536 | bytes 151875696 | solution.py:210
  197.7 24.3 %reduce-scatter.2.cloned.1.call-done = bf16[1,256,512]{2,1,0:T(8,128)(2,1)} async-done(((bf16[1,256,1024]{2,1,0:T(8,128)(2,1)}), bf16[1,256,512]{2,1,0:T(8,128)(2,1)}) %reduce-scatter.2.cloned.1.call-update) | async-done | bytes 262160 | tf_op jit(solution)/shard_map/while/body/eval_jaxpr/reduce_scatter | solution.py:181
  238.4 16.3 %select_add_fusion.5 = f32[9,1024,512]{2,1,0:T(8,128)} fusion(f32[9,1024,512]{2,1,0:T(8,128)} %get-tuple-element.1632, f32[9,1024,512]{2,1,0:T(8,128)} %get-tuple-element.1584, pred[]{:T(512)S(6)} %compare.6), kind=kLoop, calls=%fused_computation.90.clone.1 | loop fusion | flops 9437184 | bytes 56623104 | tf_op jit(solution)/shard_map/while/body/eval_jaxpr/add | solution.py:161
  260.4 32.7 %reduce-scatter.2.cloned.1.call-done = bf16[1,256,512]{2,1,0:T(8,128)(2,1)} async-done(((bf16[1,256,1024]{2,1,0:T(8,128)(2,1)}), bf16[1,256,512]{2,1,0:T(8,128)(2,1)}) %reduce-scatter.2.cloned.1.call-update) | async-done | bytes 262160 | tf_op jit(solution)/shard_map/while/body/eval_jaxpr/reduce_scatter | solution.py:181
  309.5 20.4 %select_add_fusion.5 = f32[9,1024,512]{2,1,0:T(8,128)} fusion(f32[9,1024,512]{2,1,0:T(8,128)} %get-tuple-element.1632, f32[9,1024,512]{2,1,0:T(8,128)} %get-tuple-element.1584, pred[]{:T(512)S(6)} %compare.6), kind=kLoop, calls=%fused_computation.90.clone.1 | loop fusion | flops 9437184 | bytes 56623104 | tf_op jit(solution)/shard_map/while/body/eval_jaxpr/add | solution.py:161
  335.5 32.7 %reduce-scatter.2.cloned.1.call-done = bf16[1,256,512]{2,1,0:T(8,128)(2,1)} async-done(((bf16[1,256,1024]{2,1,0:T(8,128)(2,1)}), bf16[1,256,512]{2,1,0:T(8,128)(2,1)}) %reduce-scatter.2.cloned.1.call-update) | async-done | bytes 262160 | tf_op jit(solution)/shard_map/while/body/eval_jaxpr/reduce_scatter | solution.py:181
  384.6 20.4 %select_add_fusion.5 = f32[9,1024,512]{2,1,0:T(8,128)} fusion(f32[9,1024,512]{2,1,0:T(8,128)} %get-tuple-element.1632, f32[9,1024,512]{2,1,0:T(8,128)} %get-tuple-element.1584, pred[]{:T(512)S(6)} %compare.6), kind=kLoop, calls=%fused_computation.90.clone.1 | loop fusion | flops 9437184 | bytes 56623104 | tf_op jit(solution)/shard_map/while/body/eval_jaxpr/add | solution.py:161
  417.4 25.9 %reduce-scatter.2.cloned.1.call-done = bf16[1,256,512]{2,1,0:T(8,128)(2,1)} async-done(((bf16[1,256,1024]{2,1,0:T(8,128)(2,1)}), bf16[1,256,512]{2,1,0:T(8,128)(2,1)}) %reduce-scatter.2.cloned.1.call-update) | async-done | bytes 262160 | tf_op jit(solution)/shard_map/while/body/eval_jaxpr/reduce_scatter | solution.py:181
  450.8 23.9 %conditional.10 = (f32[9,1024,512]{2,1,0:T(8,128)}) conditional(s32[]{:T(128)} %convert_element_type.629, () %tuple.162, (bf16[1,256,1024]{2,1,0:T(8,128)(2,1)S(1)}, pred[]{:T(512)}, pred[]{:T(512)}, bf16[1,1,256,512]{3,2,1,0:T(8,128)(2,1)}, bf16[1,1,256,512]{3,2,1,0:T(8,128)(2,1)S(1)}, /*index=5*/bf16[1,1,256,512]{3,2,1,0:T(8,128)(2,1)}) %tuple.163), branch_computations={%region_16.16_spmd, %region_17.17_spmd} | conditional | flops 2416181248 | bytes 54263928 | solution.py:161
  474.7 20.4 %select_add_fusion.5 = f32[9,1024,512]{2,1,0:T(8,128)} fusion(f32[9,1024,512]{2,1,0:T(8,128)} %get-tuple-element.1632, f32[9,1024,512]{2,1,0:T(8,128)} %get-tuple-element.1584, pred[]{:T(512)S(6)} %compare.6), kind=kLoop, calls=%fused_computation.90.clone.1 | loop fusion | flops 9437184 | bytes 56623104 | tf_op jit(solution)/shard_map/while/body/eval_jaxpr/add | solution.py:161
  524.2 23.9 %conditional.10 = (f32[9,1024,512]{2,1,0:T(8,128)}) conditional(s32[]{:T(128)} %convert_element_type.629, () %tuple.162, (bf16[1,256,1024]{2,1,0:T(8,128)(2,1)S(1)}, pred[]{:T(512)}, pred[]{:T(512)}, bf16[1,1,256,512]{3,2,1,0:T(8,128)(2,1)}, bf16[1,1,256,512]{3,2,1,0:T(8,128)(2,1)S(1)}, /*index=5*/bf16[1,1,256,512]{3,2,1,0:T(8,128)(2,1)}) %tuple.163), branch_computations={%region_16.16_spmd, %region_17.17_spmd} | conditional | flops 2416181248 | bytes 54263928 | solution.py:161
  548.2 20.4 %select_add_fusion.5 = f32[9,1024,512]{2,1,0:T(8,128)} fusion(f32[9,1024,512]{2,1,0:T(8,128)} %get-tuple-element.1632, f32[9,1024,512]{2,1,0:T(8,128)} %get-tuple-element.1584, pred[]{:T(512)S(6)} %compare.6), kind=kLoop, calls=%fused_computation.90.clone.1 | loop fusion | flops 9437184 | bytes 56623104 | tf_op jit(solution)/shard_map/while/body/eval_jaxpr/add | solution.py:161
  596.8 23.9 %conditional.10 = (f32[9,1024,512]{2,1,0:T(8,128)}) conditional(s32[]{:T(128)} %convert_element_type.629, () %tuple.162, (bf16[1,256,1024]{2,1,0:T(8,128)(2,1)S(1)}, pred[]{:T(512)}, pred[]{:T(512)}, bf16[1,1,256,512]{3,2,1,0:T(8,128)(2,1)}, bf16[1,1,256,512]{3,2,1,0:T(8,128)(2,1)S(1)}, /*index=5*/bf16[1,1,256,512]{3,2,1,0:T(8,128)(2,1)}) %tuple.163), branch_computations={%region_16.16_spmd, %region_17.17_spmd} | conditional | flops 2416181248 | bytes 54263928 | solution.py:161
  620.7 20.4 %select_add_fusion.5 = f32[9,1024,512]{2,1,0:T(8,128)} fusion(f32[9,1024,512]{2,1,0:T(8,128)} %get-tuple-element.1632, f32[9,1024,512]{2,1,0:T(8,128)} %get-tuple-element.1584, pred[]{:T(512)S(6)} %compare.6), kind=kLoop, calls=%fused_computation.90.clone.1 | loop fusion | flops 9437184 | bytes 56623104 | tf_op jit(solution)/shard_map/while/body/eval_jaxpr/add | solution.py:161
  667.2 23.9 %conditional.10 = (f32[9,1024,512]{2,1,0:T(8,128)}) conditional(s32[]{:T(128)} %convert_element_type.629, () %tuple.162, (bf16[1,256,1024]{2,1,0:T(8,128)(2,1)S(1)}, pred[]{:T(512)}, pred[]{:T(512)}, bf16[1,1,256,512]{3,2,1,0:T(8,128)(2,1)}, bf16[1,1,256,512]{3,2,1,0:T(8,128)(2,1)S(1)}, /*index=5*/bf16[1,1,256,512]{3,2,1,0:T(8,128)(2,1)}) %tuple.163), branch_computations={%region_16.16_spmd, %region_17.17_spmd} | conditional | flops 2416181248 | bytes 54263928 | solution.py:161
  691.2 20.4 %select_add_fusion.5 = f32[9,1024,512]{2,1,0:T(8,128)} fusion(f32[9,1024,512]{2,1,0:T(8,128)} %get-tuple-element.1632, f32[9,1024,512]{2,1,0:T(8,128)} %get-tuple-element.1584, pred[]{:T(512)S(6)} %compare.6), kind=kLoop, calls=%fused_computation.90.clone.1 | loop fusion | flops 9437184 | bytes 56623104 | tf_op jit(solution)/shard_map/while/body/eval_jaxpr/add | solution.py:161
  713.4 11.5 %convert_bitcast_fusion.3 = bf16[1,9,1024,512]{3,2,1,0:T(8,128)(2,1)} fusion(f32[9,1024,512]{2,1,0:T(8,128)} %get-tuple-element.1057), kind=kLoop, calls=%fused_computation.129 | loop fusion | flops 4718592 | bytes 28311552 | tf_op jit(solution)/shard_map/broadcast_in_dim | solution.py:216
  736.4 175.3 %all-reduce.6.cloned.1.call-done = bf16[1,9,1024,512]{3,2,1,0:T(8,128)(2,1)} async-done(((bf16[1,9,1024,512]{3,2,1,0:T(8,128)(2,1)}), bf16[1,9,1024,512]{3,2,1,0:T(8,128)(2,1)}) %all-reduce.6.cloned.1.call-update) | async-done | bytes 9437200 | tf_op jit(solution)/shard_map/psum | solution.py:212
  911.7 13.1 %broadcast_in_dim.125 = f32[1,9,1024,512]{3,2,1,0:T(8,128)} convert(bf16[1,9,1024,512]{3,2,1,0:T(8,128)(2,1)} %all-reduce.6.cloned.1.call-done) | non-fusion elementwise | flops 4718592 | bytes 28311552 | tf_op jit(solution)/shard_map/broadcast_in_dim | solution.py:216
  (642 shorter events, 496.5 us)
Async XLA Ops:
  20.4 13.3 %collective-permute-start = (bf16[2,1,256,512]{3,2,1,0:T(8,128)(2,1)S(1)}, bf16[2,1,256,512]{3,2,1,0:T(8,128)(2,1)S(1)}, u32[]{:S(2)}, u32[]{:S(2)}) collective-permute-start(bf16[2,1,256,512]{3,2,1,0:T(8,128)(2,1)S(1)} %fusion.65), channel_id=1, source_target_pairs={{0,2},{2,4},{4,6},{1,3},{3,5},{5,7},{8,10},{10,12},{12,14},{9,11},... | collective-permute-start | bytes 1572872 | tf_op jit(solution)/shard_map/while/body/eval_jaxpr/ppermute | solution.py:16
  45.9 15.9 %collective-permute-start = (bf16[2,1,256,512]{3,2,1,0:T(8,128)(2,1)S(1)}, bf16[2,1,256,512]{3,2,1,0:T(8,128)(2,1)S(1)}, u32[]{:S(2)}, u32[]{:S(2)}) collective-permute-start(bf16[2,1,256,512]{3,2,1,0:T(8,128)(2,1)S(1)} %fusion.65), channel_id=1, source_target_pairs={{0,2},{2,4},{4,6},{1,3},{3,5},{5,7},{8,10},{10,12},{12,14},{9,11},... | collective-permute-start | bytes 1572872 | tf_op jit(solution)/shard_map/while/body/eval_jaxpr/ppermute | solution.py:16
  74.0 15.9 %collective-permute-start = (bf16[2,1,256,512]{3,2,1,0:T(8,128)(2,1)S(1)}, bf16[2,1,256,512]{3,2,1,0:T(8,128)(2,1)S(1)}, u32[]{:S(2)}, u32[]{:S(2)}) collective-permute-start(bf16[2,1,256,512]{3,2,1,0:T(8,128)(2,1)S(1)} %fusion.65), channel_id=1, source_target_pairs={{0,2},{2,4},{4,6},{1,3},{3,5},{5,7},{8,10},{10,12},{12,14},{9,11},... | collective-permute-start | bytes 1572872 | tf_op jit(solution)/shard_map/while/body/eval_jaxpr/ppermute | solution.py:16
  102.0 15.9 %collective-permute-start = (bf16[2,1,256,512]{3,2,1,0:T(8,128)(2,1)S(1)}, bf16[2,1,256,512]{3,2,1,0:T(8,128)(2,1)S(1)}, u32[]{:S(2)}, u32[]{:S(2)}) collective-permute-start(bf16[2,1,256,512]{3,2,1,0:T(8,128)(2,1)S(1)} %fusion.65), channel_id=1, source_target_pairs={{0,2},{2,4},{4,6},{1,3},{3,5},{5,7},{8,10},{10,12},{12,14},{9,11},... | collective-permute-start | bytes 1572872 | tf_op jit(solution)/shard_map/while/body/eval_jaxpr/ppermute | solution.py:16
  123.2 22.7 %collective-permute-start = (bf16[2,1,256,512]{3,2,1,0:T(8,128)(2,1)S(1)}, bf16[2,1,256,512]{3,2,1,0:T(8,128)(2,1)S(1)}, u32[]{:S(2)}, u32[]{:S(2)}) collective-permute-start(bf16[2,1,256,512]{3,2,1,0:T(8,128)(2,1)S(1)} %fusion.65), channel_id=1, source_target_pairs={{0,2},{2,4},{4,6},{1,3},{3,5},{5,7},{8,10},{10,12},{12,14},{9,11},... | collective-permute-start | bytes 1572872 | tf_op jit(solution)/shard_map/while/body/eval_jaxpr/ppermute | solution.py:16
  151.3 15.9 %collective-permute-start = (bf16[2,1,256,512]{3,2,1,0:T(8,128)(2,1)S(1)}, bf16[2,1,256,512]{3,2,1,0:T(8,128)(2,1)S(1)}, u32[]{:S(2)}, u32[]{:S(2)}) collective-permute-start(bf16[2,1,256,512]{3,2,1,0:T(8,128)(2,1)S(1)} %fusion.65), channel_id=1, source_target_pairs={{0,2},{2,4},{4,6},{1,3},{3,5},{5,7},{8,10},{10,12},{12,14},{9,11},... | collective-permute-start | bytes 1572872 | tf_op jit(solution)/shard_map/while/body/eval_jaxpr/ppermute | solution.py:16
  172.5 20.5 %collective-permute-start = (bf16[2,1,256,512]{3,2,1,0:T(8,128)(2,1)S(1)}, bf16[2,1,256,512]{3,2,1,0:T(8,128)(2,1)S(1)}, u32[]{:S(2)}, u32[]{:S(2)}) collective-permute-start(bf16[2,1,256,512]{3,2,1,0:T(8,128)(2,1)S(1)} %fusion.65), channel_id=1, source_target_pairs={{0,2},{2,4},{4,6},{1,3},{3,5},{5,7},{8,10},{10,12},{12,14},{9,11},... | collective-permute-start | bytes 1572872 | tf_op jit(solution)/shard_map/while/body/eval_jaxpr/ppermute | solution.py:16
  193.9 28.1 %reduce-scatter.2.cloned.1.call-start = ((), (), s32[]{:S(2)}) async-start(), calls=%async_computation.2 | async-start | bytes 786432 | tf_op jit(solution)/shard_map/while/body/eval_jaxpr/reduce_scatter | solution.py:181
  228.2 26.5 %collective-permute-start.1 = (bf16[2,1,256,512]{3,2,1,0:T(8,128)(2,1)}, bf16[2,1,256,512]{3,2,1,0:T(8,128)(2,1)}, u32[]{:S(2)}, u32[]{:S(2)}) collective-permute-start(bf16[2,1,256,512]{3,2,1,0:T(8,128)(2,1)} %fusion.69), channel_id=1, source_target_pairs={{2,0},{4,2},{6,4},{3,1},{5,3},{7,5},{10,8},{12,10},{14,12},{11,9},... | collective-permute-start | bytes 1572872 | tf_op jit(solution)/shard_map/while/body/eval_jaxpr/ppermute | solution.py:16
  256.6 36.5 %reduce-scatter.2.cloned.1.call-start = ((), (), s32[]{:S(2)}) async-start(), calls=%async_computation.2 | async-start | bytes 786432 | tf_op jit(solution)/shard_map/while/body/eval_jaxpr/reduce_scatter | solution.py:181
  259.1 33.9 %copy-start.7 = (f32[1,512]{1,0:T(1,128)S(1)}, f32[1,512]{1,0:T(1,128)}, u32[]{:S(2)}) copy-start(f32[1,512]{1,0:T(1,128)} %get-tuple-element.1623) | copy-start | bytes 6148 | tf_op jit(solution)/shard_map/while
  259.1 33.9 %copy-start.8 = (f32[1,512]{1,0:T(1,128)S(1)}, f32[1,512]{1,0:T(1,128)}, u32[]{:S(2)}) copy-start(f32[1,512]{1,0:T(1,128)} %get-tuple-element.1624) | copy-start | bytes 6148 | tf_op jit(solution)/shard_map/while
  299.3 30.6 %collective-permute-start.1 = (bf16[2,1,256,512]{3,2,1,0:T(8,128)(2,1)}, bf16[2,1,256,512]{3,2,1,0:T(8,128)(2,1)}, u32[]{:S(2)}, u32[]{:S(2)}) collective-permute-start(bf16[2,1,256,512]{3,2,1,0:T(8,128)(2,1)} %fusion.69), channel_id=1, source_target_pairs={{2,0},{4,2},{6,4},{3,1},{5,3},{7,5},{10,8},{12,10},{14,12},{11,9},... | collective-permute-start | bytes 1572872 | tf_op jit(solution)/shard_map/while/body/eval_jaxpr/ppermute | solution.py:16
  331.7 36.5 %reduce-scatter.2.cloned.1.call-start = ((), (), s32[]{:S(2)}) async-start(), calls=%async_computation.2 | async-start | bytes 786432 | tf_op jit(solution)/shard_map/while/body/eval_jaxpr/reduce_scatter | solution.py:181
  374.4 30.6 %collective-permute-start.1 = (bf16[2,1,256,512]{3,2,1,0:T(8,128)(2,1)}, bf16[2,1,256,512]{3,2,1,0:T(8,128)(2,1)}, u32[]{:S(2)}, u32[]{:S(2)}) collective-permute-start(bf16[2,1,256,512]{3,2,1,0:T(8,128)(2,1)} %fusion.69), channel_id=1, source_target_pairs={{2,0},{4,2},{6,4},{3,1},{5,3},{7,5},{10,8},{12,10},{14,12},{11,9},... | collective-permute-start | bytes 1572872 | tf_op jit(solution)/shard_map/while/body/eval_jaxpr/ppermute | solution.py:16
  406.8 36.5 %reduce-scatter.2.cloned.1.call-start = ((), (), s32[]{:S(2)}) async-start(), calls=%async_computation.2 | async-start | bytes 786432 | tf_op jit(solution)/shard_map/while/body/eval_jaxpr/reduce_scatter | solution.py:181
  449.5 45.6 %collective-permute-start.1 = (bf16[2,1,256,512]{3,2,1,0:T(8,128)(2,1)}, bf16[2,1,256,512]{3,2,1,0:T(8,128)(2,1)}, u32[]{:S(2)}, u32[]{:S(2)}) collective-permute-start(bf16[2,1,256,512]{3,2,1,0:T(8,128)(2,1)} %fusion.69), channel_id=1, source_target_pairs={{2,0},{4,2},{6,4},{3,1},{5,3},{7,5},{10,8},{12,10},{14,12},{11,9},... | collective-permute-start | bytes 1572872 | tf_op jit(solution)/shard_map/while/body/eval_jaxpr/ppermute | solution.py:16
  497.0 19.8 %reduce-scatter.2.cloned.1.call-start = ((), (), s32[]{:S(2)}) async-start(), calls=%async_computation.2 | async-start | bytes 786432 | tf_op jit(solution)/shard_map/while/body/eval_jaxpr/reduce_scatter | solution.py:181
  522.9 45.6 %collective-permute-start.1 = (bf16[2,1,256,512]{3,2,1,0:T(8,128)(2,1)}, bf16[2,1,256,512]{3,2,1,0:T(8,128)(2,1)}, u32[]{:S(2)}, u32[]{:S(2)}) collective-permute-start(bf16[2,1,256,512]{3,2,1,0:T(8,128)(2,1)} %fusion.69), channel_id=1, source_target_pairs={{2,0},{4,2},{6,4},{3,1},{5,3},{7,5},{10,8},{12,10},{14,12},{11,9},... | collective-permute-start | bytes 1572872 | tf_op jit(solution)/shard_map/while/body/eval_jaxpr/ppermute | solution.py:16
  570.4 18.8 %reduce-scatter.2.cloned.1.call-start = ((), (), s32[]{:S(2)}) async-start(), calls=%async_computation.2 | async-start | bytes 786432 | tf_op jit(solution)/shard_map/while/body/eval_jaxpr/reduce_scatter | solution.py:181
  595.5 45.6 %collective-permute-start.1 = (bf16[2,1,256,512]{3,2,1,0:T(8,128)(2,1)}, bf16[2,1,256,512]{3,2,1,0:T(8,128)(2,1)}, u32[]{:S(2)}, u32[]{:S(2)}) collective-permute-start(bf16[2,1,256,512]{3,2,1,0:T(8,128)(2,1)} %fusion.69), channel_id=1, source_target_pairs={{2,0},{4,2},{6,4},{3,1},{5,3},{7,5},{10,8},{12,10},{14,12},{11,9},... | collective-permute-start | bytes 1572872 | tf_op jit(solution)/shard_map/while/body/eval_jaxpr/ppermute | solution.py:16
  643.0 16.8 %reduce-scatter.2.cloned.1.call-start = ((), (), s32[]{:S(2)}) async-start(), calls=%async_computation.2 | async-start | bytes 786432 | tf_op jit(solution)/shard_map/while/body/eval_jaxpr/reduce_scatter | solution.py:181
  665.9 45.6 %collective-permute-start.1 = (bf16[2,1,256,512]{3,2,1,0:T(8,128)(2,1)}, bf16[2,1,256,512]{3,2,1,0:T(8,128)(2,1)}, u32[]{:S(2)}, u32[]{:S(2)}) collective-permute-start(bf16[2,1,256,512]{3,2,1,0:T(8,128)(2,1)} %fusion.69), channel_id=1, source_target_pairs={{2,0},{4,2},{6,4},{3,1},{5,3},{7,5},{10,8},{12,10},{14,12},{11,9},... | collective-permute-start | bytes 1572872 | tf_op jit(solution)/shard_map/while/body/eval_jaxpr/ppermute | solution.py:16
  713.4 198.3 %all-reduce.6.cloned.1.call-start = ((), (), s32[]{:S(2)}) async-start(), calls=%async_computation.1 | async-start | bytes 18874368 | tf_op jit(solution)/shard_map/psum | solution.py:212
  (53 other events, 558.5 us)
Sparse Core Ops, SparseCore 0:
  197.5 24.4 reduce-scatter.1
  260.2 32.8 reduce-scatter.1
  335.3 32.8 reduce-scatter.1
  417.2 26.0 reduce-scatter.1
  507.4 9.3 reduce-scatter.1
  580.8 8.4 reduce-scatter.1
  653.3 6.3 reduce-scatter.1
Sparse Core Ops, SparseCore 1:
  725.0 186.6 all-reduce.5
where the time goes:
time: 936 us; the launch traced here: 932 us
  waiting for transfers between devices  395 us (42%)
  other arithmetic  225 us (24%)
  local copies, waits for them, and re-layouts  138 us (15%)
  matrix products  66.9 us (7%)
  starting transfers between devices  48.3 us (5%)
  blocking collectives  40.9 us (4%)
  between operations  15.6 us (2%)
    psum x1, waiting for transfers between devices, local(): lax.psum(backward_state[1].astype(jnp.bfloat16), 'dp').astype(jnp.float32)  175 us
    reduce_scatter x7, waiting for transfers between devices, backward_tick(): lax.psum_scatter(partial_grad.reshape(images, pixels, full_width).astype(...  139 us
    add x7, other arithmetic, backward_tick(): grad_weight + lax.cond(active, lambda: jnp.einsum('trc,ro->tco', shifted_...  138 us
    ppermute x14, waiting for transfers between devices, shifted(): return lax.ppermute(shard, axis, pairs)  80.4 us
    ppermute x14, starting transfers between devices, shifted(): return lax.ppermute(shard, axis, pairs)  48.3 us
    reshape x32, local copies, waits for them, and re-layouts, shifted_stack(): return jnp.stack(tap_list)  35.2 us
    cond x136, local copies, waits for them, and re-layouts  33 us
    dot_general x4, matrix products, backward_tick(): jnp.einsum('trc,ro->tco', shifted_stack(shard_piece, True), grad_rows, pr...  31.3 us
  transfers between devices with their start and end apart: 22, of which 15 were waited for; matrix products, arithmetic and copies ran while one was open for 28% of the time, Pallas kernels for 0%

commit v1 on v0

v1 whole, which is shorter than its diff:
```python
import functools

import jax
import jax.numpy as jnp
from jax import lax
from jax.experimental import pallas as pl
from jax.experimental.pallas import tpu as pltpu
from jax.sharding import PartitionSpec as P

GROUPS = 32
SIDE = 16
PIXELS = SIDE * SIDE
EPSILON = 1e-05
F32 = jnp.float32
BF16 = jnp.bfloat16
MESH = pl.DeviceIdType.MESH
LIMIT = 60 * 1024 * 1024


def row_sums(values):
    return jnp.sum(values.reshape(-1, 8, values.shape[1]), axis=0)


def group_spread(partial, group_width):
    width = partial.shape[1]
    total = jnp.broadcast_to(jnp.sum(partial, axis=0, keepdims=True), partial.shape)
    lane = lax.broadcasted_iota(jnp.int32, partial.shape, 1)
    step = 1
    while step < group_width:
        above = pltpu.roll(total, width - step, 1)
        below = pltpu.roll(total, step, 1)
        total = total + jnp.where((lane & step) != 0, below, above)
        step *= 2
    return total[0:1]


def fill_shifts(dst, piece, offset, stride, forward):
    width = piece.shape[1]
    values = piece.astype(F32)
    column = lax.broadcasted_iota(jnp.int32, (PIXELS, width), 0) % SIDE
    for tap_x in range(3):
        by = tap_x - 1 if forward else 1 - tap_x
        if by == 0:
            moved = piece
        elif by == 1:
            moved = jnp.where(column < SIDE - 1, pltpu.roll(values, PIXELS - 1, 0), 0.0).astype(BF16)
        else:
            moved = jnp.where(column > 0, pltpu.roll(values, 1, 0), 0.0).astype(BF16)
        start = pl.multiple_of(tap_x * stride + offset, 128)
        dst[SIDE : SIDE + PIXELS, pl.ds(start, width)] = moved


def pipeline_kernel(
    segments, chans, copies, micros, group_width,
    x_ref, dout_ref, w_ref, gain_ref, bias_ref,
    hall, dyall, dgain_ref, dbias_ref,
    fin, yout, bin_, bout, abuf, mean_buf, rstd_buf, hx, dyx, psend, precv, stat,
    fs_send, fs_recv, bs_send, bs_recv, hc_send, hc_recv, hd_send, hd_recv,
    hf_send, hf_recv, dd_send, dd_recv, pc_send, pc_recv, st_send, st_recv,
):
    half = segments // 2
    p = lax.axis_index("segment")
    me = lax.axis_index("chan")
    img = lax.axis_index("dp")
    width = w_ref.shape[2]
    full = w_ref.shape[1]
    count = float(PIXELS * group_width)
    own = pl.ds(pl.multiple_of(me * width, 128), width)

    def chan_peer(r):
        return lax.rem(me + r, chans)

    def dp_peer(r):
        return lax.rem(img + r, copies)

    barrier = pltpu.get_barrier_semaphore()

    def greet(where):
        pl.semaphore_signal(barrier, inc=1, device_id=where, device_id_type=MESH)

    for r in range(1, chans):
        greet({"chan": chan_peer(r)})
    for r in range(1, copies):
        greet({"dp": dp_peer(r)})

    @pl.when(p > 0)
    def _():
        greet({"segment": p - 1})

    @pl.when(p < segments - 1)
    def _():
        greet({"segment": p + 1})

    neighbours = (p > 0).astype(jnp.int32) + (p < segments - 1).astype(jnp.int32)
    pl.semaphore_wait(barrier, chans - 1 + copies - 1 + neighbours)

    hx[0:SIDE, :] = jnp.zeros((SIDE, hx.shape[1]), BF16)
    hx[SIDE + PIXELS :, :] = jnp.zeros((SIDE, hx.shape[1]), BF16)
    dyx[0:SIDE, :] = jnp.zeros((SIDE, dyx.shape[1]), BF16)
    dyx[SIDE + PIXELS :, :] = jnp.zeros((SIDE, dyx.shape[1]), BF16)
    stat[img] = jnp.zeros(stat.shape[1:], F32)

    def remote(src, dst, send, recv, where):
        return pltpu.make_async_remote_copy(
            src_ref=src, dst_ref=dst, send_sem=send, recv_sem=recv,
            device_id=where, device_id_type=MESH,
        )

    class Lane:
        def __init__(self, q, by, slots, outs, send, recv):
            self.q, self.slots, self.outs, self.send, self.recv = q, slots, outs, send, recv
            self.to = {"segment": jnp.clip(p + by, 0, segments - 1)}
            self.early = q < half
            self.lev = segments - 1 - q
            self.in_slot = jnp.where(self.early, jnp.maximum(q - 1, 0), self.lev)
            self.lower = jnp.maximum(self.lev - 1, 0)
            self.low_slot = jnp.minimum(self.lower, half - 1)
            self.out_slot = jnp.where(self.early, q, self.low_slot)
            self.arrive = jnp.where(self.early, q, self.lev + 1)
            self.onward = jnp.where(self.early, q, self.lower)
            self.sends = q < segments - 1

        def pass_on(self, m, k):
            slot = self.slots.at[m, k]
            return remote(slot, slot, self.send.at[m, k], self.recv.at[m, k], self.to)

        def put(self, m):
            return remote(
                self.outs.at[m], self.slots.at[m, self.out_slot],
                self.send.at[m, self.out_slot], self.recv.at[m, self.out_slot], self.to,
            )

        def take(self, m):
            for k in range(half):
                @pl.when(k < self.arrive)
                def _():
                    self.pass_on(m, k).wait_recv()

                @pl.when(k < self.onward)
                def _():
                    self.pass_on(m, k).start()

        def give(self, m, value):
            @pl.when(self.sends)
            def _():
                @pl.when(self.early)
                def _():
                    self.outs[m] = value

                @pl.when(jnp.logical_not(self.early))
                def _():
                    skip = self.slots[m, self.low_slot].astype(F32)
                    self.outs[m] = (value.astype(F32) + skip).astype(BF16)

                self.put(m).start()

        def finish(self, m):
            @pl.when(self.sends)
            def _():
                self.put(m).wait_send()

            for k in range(half):
                @pl.when(k < self.onward)
                def _():
                    self.pass_on(m, k).wait_send()

    up = Lane(p, 1, fin, yout, fs_send, fs_recv)
    back = Lane(segments - 1 - p, -1, bin_, bout, bs_send, bs_recv)

    def h_chan(m, r):
        piece = hall.at[m, img, :, own]
        return remote(piece, piece, hc_send.at[m, r], hc_recv.at[m, r], {"chan": chan_peer(r)})

    def h_dp(m, r):
        piece = hall.at[m, img, :, own]
        return remote(piece, piece, hd_send.at[m, r], hd_recv.at[m, r], {"dp": dp_peer(r)})

    def h_fan(m, r, c):
        piece = hall.at[m, lax.rem(img - r + copies, copies), :, own]
        return remote(piece, piece, hf_send.at[m, r, c], hf_recv.at[m, r, c], {"chan": chan_peer(c)})

    def dy_dp(m, r):
        piece = dyall.at[m, img]
        return remote(piece, piece, dd_send.at[m, r], dd_recv.at[m, r], {"dp": dp_peer(r)})

    def part(m, r):
        return remote(
            psend.at[m, r], precv.at[m, r], pc_send.at[m, r], pc_recv.at[m, r],
            {"chan": chan_peer(r)},
        )

    def forward(m):
        @pl.when(p == 0)
        def _():
            abuf[m] = x_ref[m]

        @pl.when(p > 0)
        def _():
            up.take(m)
            abuf[m] = fin[m, up.in_slot]

        values = abuf[m].astype(F32)
        mean = group_spread(row_sums(values), group_width) / count
        centred = values - mean
        var = group_spread(row_sums(centred * centred), group_width) / count
        rstd = lax.rsqrt(var + EPSILON)
        mean_buf[m] = jnp.broadcast_to(mean, (8, width))
        rstd_buf[m] = jnp.broadcast_to(rstd, (8, width))
        pre = centred * rstd * gain_ref[...] + bias_ref[...]
        hall[m, img, :, own] = (pre * jax.nn.sigmoid(pre)).astype(BF16)
        for r in range(1, chans):
            h_chan(m, r).start()
        for r in range(1, copies):
            h_dp(m, r).start()

        @pl.when(up.sends)
        def _():
            fill_shifts(hx, hall[m, img, :, own], me * width, full, True)

        for r in range(1, chans):
            h_chan(m, r).wait_recv()

            @pl.when(up.sends)
            def _():
                other = lax.rem(me - r + chans, chans) * width
                piece = hall[m, img, :, pl.ds(pl.multiple_of(other, 128), width)]
                fill_shifts(hx, piece, other, full, True)

        @pl.when(up.sends)
        def _():
            acc = abuf[m].astype(F32)
            for tap_y in range(3):
                acc += jnp.dot(
                    hx[tap_y * SIDE : tap_y * SIDE + PIXELS, :],
                    w_ref[3 * tap_y : 3 * tap_y + 3].reshape(3 * full, width),
                    preferred_element_type=F32,
                )
            up.give(m, acc.astype(BF16))

    def backward(m):
        @pl.when(p == segments - 1)
        def _():
            dyall[m, img] = dout_ref[m]

        @pl.when(p < segments - 1)
        def _():
            back.take(m)
            dyall[m, img] = bin_[m, back.in_slot]

        for r in range(1, copies):
            dy_dp(m, r).start()
        fill_shifts(dyx, dyall[m, img], 0, width, False)
        for r in list(range(1, chans)) + [0]:
            rows = pl.ds(pl.multiple_of(chan_peer(r) * width, 128), width)
            acc = jnp.zeros((PIXELS, width), F32)
            for tap_y in range(3):
                for tap_x in range(3):
                    acc += lax.dot_general(
                        dyx[(2 - tap_y) * SIDE : (2 - tap_y) * SIDE + PIXELS,
                            tap_x * width : (tap_x + 1) * width],
                        w_ref[3 * tap_y + tap_x, rows, :],
                        (((1,), (1,)), ((), ())),
                        preferred_element_type=F32,
                    )
            psend[m, r] = acc.astype(BF16)
            if r:
                part(m, r).start()
        grad = psend[m, 0].astype(F32)
        for r in range(1, chans):
            part(m, r).wait_recv()
            grad += precv[m, r].astype(F32)
        rstd = rstd_buf[m][0:1]
        normed = (abuf[m].astype(F32) - mean_buf[m][0:1]) * rstd
        pre = normed * gain_ref[...] + bias_ref[...]
        sigma = jax.nn.sigmoid(pre)
        grad = grad * sigma * (1.0 + pre * (1.0 - sigma))
        stat[img, 0:8] += row_sums(grad * normed)
        stat[img, 8:16] += row_sums(grad)

        @pl.when(back.sends)
        def _():
            scaled = grad * gain_ref[...]
            first = group_spread(row_sums(scaled), group_width) / count
            second = group_spread(row_sums(scaled * normed), group_width) / count
            down = dyall[m, img].astype(F32) + rstd * (scaled - first - normed * second)
            back.give(m, down.astype(BF16))

    lag = segments - 1 - p

    def step(s, carry):
        @pl.when(s < micros)
        def _():
            forward(jnp.minimum(s, micros - 1))

        @pl.when(jnp.logical_and(s >= lag, s < lag + micros))
        def _():
            backward(jnp.clip(s - lag, 0, micros - 1))

        return carry

    lax.fori_loop(0, micros + segments - 1, step, 0)

    def stat_dp(r):
        return remote(stat.at[img], stat.at[img], st_send.at[r], st_recv.at[r], {"dp": dp_peer(r)})

    for r in range(1, copies):
        stat_dp(r).start()

    def spread(m, carry):
        for r in range(1, copies):
            h_dp(m, r).wait_recv()
            for c in range(1, chans):
                h_fan(m, r, c).start()
        return carry

    lax.fori_loop(0, micros, spread, 0)
    for r in range(1, copies):
        stat_dp(r).wait_recv()
    total = stat[0]
    for d in range(1, copies):
        total = total + stat[d]
    dgain_ref[...] = jnp.sum(total[0:8], axis=0, keepdims=True)
    dbias_ref[...] = jnp.sum(total[8:16], axis=0, keepdims=True)

    def drain(m, carry):
        for r in range(1, copies):
            dy_dp(m, r).wait_recv()
            for c in range(1, chans):
                h_fan(m, r, c).wait_recv()
        for r in range(1, copies):
            dy_dp(m, r).wait_send()
            h_dp(m, r).wait_send()
            for c in range(1, chans):
                h_fan(m, r, c).wait_send()
        for r in range(1, chans):
            h_chan(m, r).wait_send()
            part(m, r).wait_send()
        up.finish(m)
        back.finish(m)
        return carry

    lax.fori_loop(0, micros, drain, 0)
    for r in range(1, copies):
        stat_dp(r).wait_send()


def weight_kernel(h_ref, dy_ref, out_ref, ht, dyx):
    micros, copies = h_ref.shape[:2]
    width = dy_ref.shape[3]
    images = micros * copies

    @pl.when(pl.program_id(0) == 0)
    def _():
        def build(i, carry):
            slab = dyx.at[i]
            slab[0:SIDE, :] = jnp.zeros((SIDE, slab.shape[1]), BF16)
            slab[SIDE + PIXELS :, :] = jnp.zeros((SIDE, slab.shape[1]), BF16)
            fill_shifts(slab, dy_ref[i // copies, i % copies], 0, width, False)
            return carry

        lax.fori_loop(0, images, build, 0)

    for i in range(images):
        ht[:, i * PIXELS : (i + 1) * PIXELS] = h_ref[i // copies, i % copies].T
    for tap_y in range(3):
        for tap_x in range(3):
            rows = dyx[:, (2 - tap_y) * SIDE : (2 - tap_y) * SIDE + PIXELS,
                       tap_x * width : (tap_x + 1) * width]
            out_ref[3 * tap_y + tap_x] = jnp.dot(
                ht[...], rows.reshape(images * PIXELS, width), preferred_element_type=F32
            )


def local(segments, chans, copies, x_input, d_output, weights, gains, biases):
    micros, images, pixels, width = x_input.shape
    taps, full = weights.shape[1:3]
    half = segments // 2
    group_width = full // GROUPS
    vmem = pl.BlockSpec(memory_space=pltpu.VMEM)
    dma = pltpu.SemaphoreType.DMA
    act = (pixels, width)
    hall, dyall, dgain, dbias = pl.pallas_call(
        functools.partial(pipeline_kernel, segments, chans, copies, micros, group_width),
        out_shape=[
            jax.ShapeDtypeStruct((micros, copies, pixels, full), BF16),
            jax.ShapeDtypeStruct((micros, copies, pixels, width), BF16),
            jax.ShapeDtypeStruct((1, width), F32),
            jax.ShapeDtypeStruct((1, width), F32),
        ],
        in_specs=[vmem] * 5,
        out_specs=[vmem] * 4,
        scratch_shapes=[
            pltpu.VMEM((micros, half) + act, BF16),
            pltpu.VMEM((micros,) + act, BF16),
            pltpu.VMEM((micros, half) + act, BF16),
            pltpu.VMEM((micros,) + act, BF16),
            pltpu.VMEM((micros,) + act, BF16),
            pltpu.VMEM((micros, 8, width), F32),
            pltpu.VMEM((micros, 8, width), F32),
            pltpu.VMEM((pixels + 2 * SIDE, 3 * full), BF16),
            pltpu.VMEM((pixels + 2 * SIDE, 3 * width), BF16),
            pltpu.VMEM((micros, chans) + act, BF16),
            pltpu.VMEM((micros, chans) + act, BF16),
            pltpu.VMEM((copies, 16, width), F32),
            dma((micros, half)), dma((micros, half)),
            dma((micros, half)), dma((micros, half)),
            dma((micros, chans)), dma((micros, chans)),
            dma((micros, copies)), dma((micros, copies)),
            dma((micros, copies, chans)), dma((micros, copies, chans)),
            dma((micros, copies)), dma((micros, copies)),
            dma((micros, chans)), dma((micros, chans)),
            dma((copies,)), dma((copies,)),
        ],
        compiler_params=pltpu.CompilerParams(
            collective_id=0, has_side_effects=True, vmem_limit_bytes=LIMIT
        ),
        name="pipeline",
    )(
        x_input.reshape(micros, pixels, width),
        d_output.reshape(micros, pixels, width),
        weights[0], gains, biases,
    )
    block = min(256, full)
    dw = pl.pallas_call(
        weight_kernel,
        grid=(full // block,),
        out_shape=jax.ShapeDtypeStruct((taps, full, width), F32),
        in_specs=[
            pl.BlockSpec((micros, copies, pixels, block), lambda i: (0, 0, 0, i)),
            pl.BlockSpec((micros, copies, pixels, width), lambda i: (0, 0, 0, 0)),
        ],
        out_specs=pl.BlockSpec((taps, block, width), lambda i: (0, i, 0)),
        scratch_shapes=[
            pltpu.VMEM((block, micros * copies * pixels), BF16),
            pltpu.VMEM((micros * copies, pixels + 2 * SIDE, 3 * width), BF16),
        ],
        compiler_params=pltpu.CompilerParams(vmem_limit_bytes=LIMIT),
        name="weight_grad",
    )(hall, dyall)
    return (dw[None], dgain, dbias)


def solution(mesh):
    in_specs = (
        P(None, "dp", None, "chan"),
        P(None, "dp", None, "chan"),
        P("segment", None, None, "chan"),
        P("segment", "chan"),
        P("segment", "chan"),
    )
    out_specs = (P("segment", None, None, "chan"), P("segment", "chan"), P("segment", "chan"))
    body = functools.partial(
        local, mesh.shape["segment"], mesh.shape["chan"], mesh.shape["dp"]
    )
    return jax.shard_map(body, mesh=mesh, in_specs=in_specs, out_specs=out_specs, check_vma=False)
```

time: 936 us -> 211 us (0.23)
  waiting for transfers between devices: 395 us -> 0 us
  other arithmetic: 225 us -> 0 us
  Pallas kernels: 0 us -> 209 us
  local copies, waits for them, and re-layouts: 138 us -> 1.16 us
  matrix products: 66.9 us -> 0 us
  starting transfers between devices: 48.3 us -> 0 us
  blocking collectives: 40.9 us -> 0 us
  between operations: 15.6 us -> 0.66 us
    pallas_call x0 -> x2, Pallas kernels: none -> 209 us  [the longest x1 162 us: local(): pl.pallas_call(functools.partial(pipeline_kernel, segments, chans, copies...]
    psum x1 -> x0, waiting for transfers between devices: 175 us -> none  [local(): lax.psum(backward_state[1].astype(jnp.bfloat16), 'dp').astype(jnp.float32)]
    reduce_scatter x7 -> x0, waiting for transfers between devices: 139 us -> none  [backward_tick(): lax.psum_scatter(partial_grad.reshape(images, pixels, full_width).astype(...]
    add x14 -> x0, other arithmetic: 138 us -> none  [the longest x7 138 us: backward_tick(): grad_weight + lax.cond(active, lambda: jnp.einsum('trc,ro->tco', shifted_...]
    ppermute x14 -> x0, waiting for transfers between devices: 80.4 us -> none  [shifted(): return lax.ppermute(shard, axis, pairs)]
    dot_general x12 -> x0, matrix products: 66.9 us -> none  [the longest x4 31.3 us: backward_tick(): jnp.einsum('trc,ro->tco', shifted_stack(shard_piece, True), grad_rows, pr...]
    ppermute x14 -> x0, starting transfers between devices: 48.3 us -> none  [shifted(): return lax.ppermute(shard, axis, pairs)]
    reshape x32 -> x0, local copies, waits for them, and re-layouts: 35.2 us -> none  [shifted_stack(): return jnp.stack(tap_list)]
  transfers between devices with their start and end apart: 22 -> 0, of which waited for: 15 -> 0; matrix products, arithmetic and copies ran while one was open for 28% -> 0% of each run, Pallas kernels for 0% -> 0%
where the time goes in v1:
time: 211 us
  Pallas kernels  209 us (99%)
    pallas_call x1, Pallas kernels, local(): pl.pallas_call(functools.partial(pipeline_kernel, segments, chans, copies...  162 us
    pallas_call x1, Pallas kernels, local(): pl.pallas_call(weight_kernel, grid=(full // block,), out_shape=jax.ShapeD...  47.4 us

profile of v1, /device:TPU:0, one launch (start us, length us, event | category | flops | bytes accessed | tf_op | source)
XLA Modules:
  0.0 211.0 jit_solution(4272098317739975896)
XLA Ops:
  0.6 161.8 %pipeline.1 = (bf16[4,4,256,1024]{3,2,1,0:T(8,128)(2,1)}, bf16[4,4,256,512]{3,2,1,0:T(8,128)(2,1)}, f32[1,512]{1,0:T(1,128)}, f32[1,512]{1,0:T(1,128)}) custom-call(bf16[4,256,512]{2,1,0:T(8,128)(2,1)} %bitcast.6, bf16[4,256,512]{2,1,0:T(8,128)(2,1)} %bitcast.7, bf16[9,1024,512]{2,1,0:T(8,128)(2,1)} %bitcast.5, f32[1,512]{1,0:T(1,128)} %gain_ref.1, ...), custom_call_target="tpu_custom_call" | custom-call | tf_op jit(solution)/shard_map/pipeline/pallas_call | solution.py:382
  162.4 0.0 copy-start.1
  162.4 0.0 copy-start
  162.4 47.4 %weight_grad.1 = f32[9,1024,512]{2,1,0:T(8,128)} custom-call(bf16[4,4,256,1024]{3,2,1,0:T(8,128)(2,1)} %get-tuple-element.7.h_ref, bf16[4,4,256,512]{3,2,1,0:T(8,128)(2,1)} %get-tuple-element.8.dy_ref), custom_call_target="tpu_custom_call" | custom-call | tf_op jit(solution)/shard_map/weight_grad/pallas_call | solution.py:424
  209.8 0.0 copy-done.1
  209.8 0.6 copy.10
  210.4 0.0 copy-done
  210.4 0.6 copy.11
Async XLA Ops:
  162.4 47.4 %copy-start.1 = (f32[1,512]{1,0:T(1,128)S(1)}, f32[1,512]{1,0:T(1,128)}, u32[]{:S(2)}) copy-start(f32[1,512]{1,0:T(1,128)} %get-tuple-element.15) | copy-start | bytes 6148
  162.4 48.0 %copy-start = (f32[1,512]{1,0:T(1,128)S(1)}, f32[1,512]{1,0:T(1,128)}, u32[]{:S(2)}) copy-start(f32[1,512]{1,0:T(1,128)} %get-tuple-element.16) | copy-start | bytes 6148

commit v2 on v1

--- a/solution.py
+++ b/solution.py
@@ -14,7 +14,7 @@
 F32 = jnp.float32
 BF16 = jnp.bfloat16
 MESH = pl.DeviceIdType.MESH
-LIMIT = 60 * 1024 * 1024
+LIMIT = 62 * 1024 * 1024
 
 
 def row_sums(values):
@@ -53,10 +53,10 @@
 def pipeline_kernel(
     segments, chans, copies, micros, group_width,
     x_ref, dout_ref, w_ref, gain_ref, bias_ref,
-    hall, dyall, dgain_ref, dbias_ref,
-    fin, yout, bin_, bout, abuf, mean_buf, rstd_buf, hx, dyx, psend, precv, stat,
+    wsum_ref, hlast_ref, dylast_ref, dgain_ref, dbias_ref,
+    hall, dyall, wacc, ht, dyall_x, fin, yout, bin_, bout, abuf, mean_buf, rstd_buf, hx, dyx, psend, precv, stat,
     fs_send, fs_recv, bs_send, bs_recv, hc_send, hc_recv, hd_send, hd_recv,
-    hf_send, hf_recv, dd_send, dd_recv, pc_send, pc_recv, st_send, st_recv,
+    hf_send, hf_recv, dd_send, dd_recv, pc_send, pc_recv, st_send, st_recv, wcopy, lcopy,
 ):
     half = segments // 2
     p = lax.axis_index("segment")
@@ -98,6 +98,9 @@
     hx[SIDE + PIXELS :, :] = jnp.zeros((SIDE, hx.shape[1]), BF16)
     dyx[0:SIDE, :] = jnp.zeros((SIDE, dyx.shape[1]), BF16)
     dyx[SIDE + PIXELS :, :] = jnp.zeros((SIDE, dyx.shape[1]), BF16)
+    for d in range(copies):
+        dyall_x[d, 0:SIDE, :] = jnp.zeros((SIDE, dyx.shape[1]), BF16)
+        dyall_x[d, SIDE + PIXELS :, :] = jnp.zeros((SIDE, dyx.shape[1]), BF16)
     stat[img] = jnp.zeros(stat.shape[1:], F32)
 
     def remote(src, dst, send, recv, where):
@@ -185,7 +188,7 @@
 
     def part(m, r):
         return remote(
-            psend.at[m, r], precv.at[m, r], pc_send.at[m, r], pc_recv.at[m, r],
+            psend.at[m, r], precv.at[m, r - 1], pc_send.at[m, r], pc_recv.at[m, r],
             {"chan": chan_peer(r)},
         )
 
@@ -237,7 +240,7 @@
                 )
             up.give(m, acc.astype(BF16))
 
-    def backward(m):
+    def input_partials(m):
         @pl.when(p == segments - 1)
         def _():
             dyall[m, img] = dout_ref[m]
@@ -265,10 +268,12 @@
             psend[m, r] = acc.astype(BF16)
             if r:
                 part(m, r).start()
+
+    def backward(m):
         grad = psend[m, 0].astype(F32)
         for r in range(1, chans):
             part(m, r).wait_recv()
-            grad += precv[m, r].astype(F32)
+            grad += precv[m, r - 1].astype(F32)
         rstd = rstd_buf[m][0:1]
         normed = (abuf[m].astype(F32) - mean_buf[m][0:1]) * rstd
         pre = normed * gain_ref[...] + bias_ref[...]
@@ -285,20 +290,87 @@
             down = dyall[m, img].astype(F32) + rstd * (scaled - first - normed * second)
             back.give(m, down.astype(BF16))
 
+    block = ht.shape[0]
+
+    def gathered(j):
+        for r in range(1, copies):
+            h_dp(j, r).wait_recv()
+            for c in range(1, chans):
+                h_fan(j, r, c).start()
+        for r in range(1, copies):
+            dy_dp(j, r).wait_recv()
+            for c in range(1, chans):
+                h_fan(j, r, c).wait_recv()
+
+    def weight_part(j):
+        gathered(j)
+
+        @pl.when(j == 0)
+        def _():
+            def clear(t, carry):
+                wacc[t] = jnp.zeros(wacc.shape[1:], F32)
+                return carry
+
+            lax.fori_loop(0, wacc.shape[0], clear, 0)
+
+        def build(d, carry):
+            fill_shifts(dyall_x.at[d], dyall[j, d], 0, width, False)
+            return carry
+
+        lax.fori_loop(0, copies, build, 0)
+
+        def rows_of(c, carry):
+            first = pl.multiple_of(c * block, block)
+            for d in range(copies):
+                ht[:, d * PIXELS : (d + 1) * PIXELS] = hall[j, d, :, pl.ds(first, block)].T
+            for tap in range(9):
+                start = (2 - tap // 3) * SIDE
+                lanes = slice((tap % 3) * width, (tap % 3 + 1) * width)
+                rows = dyall_x[:, start : start + PIXELS, lanes].reshape(copies * PIXELS, width)
+                wacc[tap, pl.ds(first, block), :] += jnp.dot(
+                    ht[...], rows, preferred_element_type=F32
+                )
+            return carry
+
+        lax.fori_loop(0, full // block, rows_of, 0)
+
+        @pl.when(j == micros - 2)
+        def _():
+            pltpu.make_async_copy(wacc, wsum_ref, wcopy).start()
+
     lag = segments - 1 - p
+    last = p == segments - 1
+    start_f = jnp.where(last, micros, 0)
+    start_b = jnp.where(last, micros, lag)
+    ahead = jnp.where(p == 0, micros - 1, jnp.where(p == 1, 1, 0))
+    behind = jnp.where(p == 0, 1, 2)
 
     def step(s, carry):
-        @pl.when(s < micros)
-        def _():
-            forward(jnp.minimum(s, micros - 1))
+        @pl.when(jnp.logical_and(s >= start_f, s < start_f + micros))
+        def _():
+            forward(jnp.clip(s - start_f, 0, micros - 1))
+
+        early = s - lag - behind
+        late = s - steps + ahead
+        now_early = jnp.logical_and(early >= 0, early < ahead)
+        now_late = jnp.logical_and(late >= ahead, late < micros - 1)
+
+        @pl.when(jnp.logical_or(now_early, now_late))
+        def _():
+            weight_part(jnp.clip(jnp.where(now_late, late, early), 0, micros - 2))
 
         @pl.when(jnp.logical_and(s >= lag, s < lag + micros))
         def _():
-            backward(jnp.clip(s - lag, 0, micros - 1))
+            input_partials(jnp.clip(s - lag, 0, micros - 1))
+
+        @pl.when(jnp.logical_and(s >= start_b, s < start_b + micros))
+        def _():
+            backward(jnp.clip(s - start_b, 0, micros - 1))
 
         return carry
 
-    lax.fori_loop(0, micros + segments - 1, step, 0)
+    steps = max(micros + segments - 1, 2 * micros)
+    lax.fori_loop(0, steps + micros - 1, step, 0)
 
     def stat_dp(r):
         return remote(stat.at[img], stat.at[img], st_send.at[r], st_recv.at[r], {"dp": dp_peer(r)})
@@ -306,14 +378,11 @@
     for r in range(1, copies):
         stat_dp(r).start()
 
-    def spread(m, carry):
-        for r in range(1, copies):
-            h_dp(m, r).wait_recv()
-            for c in range(1, chans):
-                h_fan(m, r, c).start()
-        return carry
-
-    lax.fori_loop(0, micros, spread, 0)
+    gathered(micros - 1)
+    h_copy = pltpu.make_async_copy(hall.at[micros - 1], hlast_ref, lcopy.at[0])
+    dy_copy = pltpu.make_async_copy(dyall.at[micros - 1], dylast_ref, lcopy.at[1])
+    h_copy.start()
+    dy_copy.start()
     for r in range(1, copies):
         stat_dp(r).wait_recv()
     total = stat[0]
@@ -323,10 +392,6 @@
     dbias_ref[...] = jnp.sum(total[8:16], axis=0, keepdims=True)
 
     def drain(m, carry):
-        for r in range(1, copies):
-            dy_dp(m, r).wait_recv()
-            for c in range(1, chans):
-                h_fan(m, r, c).wait_recv()
         for r in range(1, copies):
             dy_dp(m, r).wait_send()
             h_dp(m, r).wait_send()
@@ -342,12 +407,14 @@
     lax.fori_loop(0, micros, drain, 0)
     for r in range(1, copies):
         stat_dp(r).wait_send()
-
-
-def weight_kernel(h_ref, dy_ref, out_ref, ht, dyx):
-    micros, copies = h_ref.shape[:2]
-    width = dy_ref.shape[3]
-    images = micros * copies
+    h_copy.wait()
+    dy_copy.wait()
+    pltpu.make_async_copy(wacc, wsum_ref, wcopy).wait()
+
+
+def weight_kernel(sum_ref, h_ref, dy_ref, out_ref, ht, dyx):
+    images = h_ref.shape[0]
+    width = dy_ref.shape[2]
 
     @pl.when(pl.program_id(0) == 0)
     def _():
@@ -355,20 +422,19 @@
             slab = dyx.at[i]
             slab[0:SIDE, :] = jnp.zeros((SIDE, slab.shape[1]), BF16)
             slab[SIDE + PIXELS :, :] = jnp.zeros((SIDE, slab.shape[1]), BF16)
-            fill_shifts(slab, dy_ref[i // copies, i % copies], 0, width, False)
+            fill_shifts(slab, dy_ref[i], 0, width, False)
             return carry
 
         lax.fori_loop(0, images, build, 0)
 
     for i in range(images):
-        ht[:, i * PIXELS : (i + 1) * PIXELS] = h_ref[i // copies, i % copies].T
-    for tap_y in range(3):
-        for tap_x in range(3):
-            rows = dyx[:, (2 - tap_y) * SIDE : (2 - tap_y) * SIDE + PIXELS,
-                       tap_x * width : (tap_x + 1) * width]
-            out_ref[3 * tap_y + tap_x] = jnp.dot(
-                ht[...], rows.reshape(images * PIXELS, width), preferred_element_type=F32
-            )
+        ht[:, i * PIXELS : (i + 1) * PIXELS] = h_ref[i].T
+    for tap in range(9):
+        start = (2 - tap // 3) * SIDE
+        rows = dyx[:, start : start + PIXELS, (tap % 3) * width : (tap % 3 + 1) * width]
+        out_ref[tap] = sum_ref[tap] + jnp.dot(
+            ht[...], rows.reshape(images * PIXELS, width), preferred_element_type=F32
+        )
 
 
 def local(segments, chans, copies, x_input, d_output, weights, gains, biases):
@@ -379,17 +445,25 @@
     vmem = pl.BlockSpec(memory_space=pltpu.VMEM)
     dma = pltpu.SemaphoreType.DMA
     act = (pixels, width)
-    hall, dyall, dgain, dbias = pl.pallas_call(
+    block = min(256, full)
+    hbm = pl.BlockSpec(memory_space=pl.ANY)
+    wsum, hlast, dylast, dgain, dbias = pl.pallas_call(
         functools.partial(pipeline_kernel, segments, chans, copies, micros, group_width),
         out_shape=[
-            jax.ShapeDtypeStruct((micros, copies, pixels, full), BF16),
-            jax.ShapeDtypeStruct((micros, copies, pixels, width), BF16),
+            jax.ShapeDtypeStruct((taps, full, width), F32),
+            jax.ShapeDtypeStruct((copies, pixels, full), BF16),
+            jax.ShapeDtypeStruct((copies, pixels, width), BF16),
             jax.ShapeDtypeStruct((1, width), F32),
             jax.ShapeDtypeStruct((1, width), F32),
         ],
         in_specs=[vmem] * 5,
-        out_specs=[vmem] * 4,
+        out_specs=[hbm] * 3 + [vmem] * 2,
         scratch_shapes=[
+            pltpu.VMEM((micros, copies, pixels, full), BF16),
+            pltpu.VMEM((micros, copies, pixels, width), BF16),
+            pltpu.VMEM((taps, full, width), F32),
+            pltpu.VMEM((block, copies * pixels), BF16),
+            pltpu.VMEM((copies, pixels + 2 * SIDE, 3 * width), BF16),
             pltpu.VMEM((micros, half) + act, BF16),
             pltpu.VMEM((micros,) + act, BF16),
             pltpu.VMEM((micros, half) + act, BF16),
@@ -400,7 +474,7 @@
             pltpu.VMEM((pixels + 2 * SIDE, 3 * full), BF16),
             pltpu.VMEM((pixels + 2 * SIDE, 3 * width), BF16),
             pltpu.VMEM((micros, chans) + act, BF16),
-            pltpu.VMEM((micros, chans) + act, BF16),
+            pltpu.VMEM((micros, chans - 1) + act, BF16),
             pltpu.VMEM((copies, 16, width), F32),
             dma((micros, half)), dma((micros, half)),
             dma((micros, half)), dma((micros, half)),
@@ -410,6 +484,7 @@
             dma((micros, copies)), dma((micros, copies)),
             dma((micros, chans)), dma((micros, chans)),
             dma((copies,)), dma((copies,)),
+            dma, dma((2,)),
         ],
         compiler_params=pltpu.CompilerParams(
             collective_id=0, has_side_effects=True, vmem_limit_bytes=LIMIT
@@ -420,23 +495,23 @@
         d_output.reshape(micros, pixels, width),
         weights[0], gains, biases,
     )
-    block = min(256, full)
     dw = pl.pallas_call(
         weight_kernel,
         grid=(full // block,),
         out_shape=jax.ShapeDtypeStruct((taps, full, width), F32),
         in_specs=[
-            pl.BlockSpec((micros, copies, pixels, block), lambda i: (0, 0, 0, i)),
-            pl.BlockSpec((micros, copies, pixels, width), lambda i: (0, 0, 0, 0)),
+            pl.BlockSpec((taps, block, width), lambda i: (0, i, 0)),
+            pl.BlockSpec((copies, pixels, block), lambda i: (0, 0, i)),
+            pl.BlockSpec((copies, pixels, width), lambda i: (0, 0, 0)),
         ],
         out_specs=pl.BlockSpec((taps, block, width), lambda i: (0, i, 0)),
         scratch_shapes=[
-            pltpu.VMEM((block, micros * copies * pixels), BF16),
-            pltpu.VMEM((micros * copies, pixels + 2 * SIDE, 3 * width), BF16),
+            pltpu.VMEM((block, copies * pixels), BF16),
+            pltpu.VMEM((copies, pixels + 2 * SIDE, 3 * width), BF16),
         ],
         compiler_params=pltpu.CompilerParams(vmem_limit_bytes=LIMIT),
         name="weight_grad",
-    )(hall, dyall)
+    )(wsum, hlast, dylast)
     return (dw[None], dgain, dbias)
 
 

time: 211 us -> 194 us (0.919)
  Pallas kernels: 209 us -> 192 us
    pallas_call x1, Pallas kernels: 47.4 us -> 19.4 us  [local(): pl.pallas_call(weight_kernel, grid=(full // block,), out_shape=jax.ShapeD...]
    pallas_call x1, Pallas kernels: 162 us -> 173 us  [local(): pl.pallas_call(functools.partial(pipeline_kernel, segments, chans, copies...]
where the time goes in v2:
time: 194 us
  Pallas kernels  192 us (99%)
    pallas_call x1, Pallas kernels, local(): pl.pallas_call(functools.partial(pipeline_kernel, segments, chans, copies...  173 us
    pallas_call x1, Pallas kernels, local(): pl.pallas_call(weight_kernel, grid=(full // block,), out_shape=jax.ShapeD...  19.4 us

profile of v2, /device:TPU:0, one launch (start us, length us, event | category | flops | bytes accessed | tf_op | source)
XLA Modules:
  0.0 193.9 jit_solution(1315890743881783350)
XLA Ops:
  0.6 172.7 %pipeline.1 = (f32[9,1024,512]{2,1,0:T(8,128)}, bf16[4,256,1024]{2,1,0:T(8,128)(2,1)}, bf16[4,256,512]{2,1,0:T(8,128)(2,1)}, f32[1,512]{1,0:T(1,128)}, f32[1,512]{1,0:T(1,128)}) custom-call(bf16[4,256,512]{2,1,0:T(8,128)(2,1)} %bitcast.6, bf16[4,256,512]{2,1,0:T(8,128)(2,1)} %bitcast.7, bf16[9,1024,512]{2,1,0:T(8,128)(2,1)} %bitcast.5, f32[1,512]{1,0:T(1,128)} %gain_ref.1, ...), custom_call_target="tpu_custom_call" | custom-call | tf_op jit(solution)/shard_map/pipeline/pallas_call | solution.py:450
  173.3 0.0 copy-start.1
  173.3 0.0 copy-start
  173.4 19.4 %weight_grad.1 = f32[9,1024,512]{2,1,0:T(8,128)} custom-call(f32[9,1024,512]{2,1,0:T(8,128)} %get-tuple-element.8.sum_ref, bf16[4,256,1024]{2,1,0:T(8,128)(2,1)} %get-tuple-element.9.h_ref, bf16[4,256,512]{2,1,0:T(8,128)(2,1)} %get-tuple-element.10.dy_ref), custom_call_target="tpu_custom_call" | custom-call | tf_op jit(solution)/shard_map/weight_grad/pallas_call | solution.py:498
  192.7 0.0 copy-done.1
  192.7 0.6 copy.10
  193.3 0.0 copy-done
  193.3 0.6 copy.11
Async XLA Ops:
  173.3 19.4 %copy-start.1 = (f32[1,512]{1,0:T(1,128)S(1)}, f32[1,512]{1,0:T(1,128)}, u32[]{:S(2)}) copy-start(f32[1,512]{1,0:T(1,128)} %get-tuple-element.17) | copy-start | bytes 6148
  173.3 19.9 %copy-start = (f32[1,512]{1,0:T(1,128)S(1)}, f32[1,512]{1,0:T(1,128)}, u32[]{:S(2)}) copy-start(f32[1,512]{1,0:T(1,128)} %get-tuple-element.18) | copy-start | bytes 6148

commit v3 on v2

--- a/solution.py
+++ b/solution.py
@@ -342,7 +342,7 @@
     last = p == segments - 1
     start_f = jnp.where(last, micros, 0)
     start_b = jnp.where(last, micros, lag)
-    ahead = jnp.where(p == 0, micros - 1, jnp.where(p == 1, 1, 0))
+    ahead = jnp.where(p == 0, micros - 2, jnp.where(p == 1, 1, 0))
     behind = jnp.where(p == 0, 1, 2)
 
     def step(s, carry):
@@ -462,7 +462,7 @@
             pltpu.VMEM((micros, copies, pixels, full), BF16),
             pltpu.VMEM((micros, copies, pixels, width), BF16),
             pltpu.VMEM((taps, full, width), F32),
-            pltpu.VMEM((block, copies * pixels), BF16),
+            pltpu.VMEM((min(512, full), copies * pixels), BF16),
             pltpu.VMEM((copies, pixels + 2 * SIDE, 3 * width), BF16),
             pltpu.VMEM((micros, half) + act, BF16),
             pltpu.VMEM((micros,) + act, BF16),

time: 194 us -> 186 us (0.959)
  Pallas kernels: 192 us -> 184 us
    pallas_call x1, Pallas kernels: 173 us -> 165 us  [local(): pl.pallas_call(functools.partial(pipeline_kernel, segments, chans, copies...]
where the time goes in v3:
time: 186 us
  Pallas kernels  184 us (99%)
    pallas_call x1, Pallas kernels, local(): pl.pallas_call(functools.partial(pipeline_kernel, segments, chans, copies...  165 us
    pallas_call x1, Pallas kernels, local(): pl.pallas_call(weight_kernel, grid=(full // block,), out_shape=jax.ShapeD...  19.4 us

profile of v3, /device:TPU:0, one launch (start us, length us, event | category | flops | bytes accessed | tf_op | source)
XLA Modules:
  0.0 185.9 jit_solution(11743080801663065568)
XLA Ops:
  0.6 164.7 %pipeline.1 = (f32[9,1024,512]{2,1,0:T(8,128)}, bf16[4,256,1024]{2,1,0:T(8,128)(2,1)}, bf16[4,256,512]{2,1,0:T(8,128)(2,1)}, f32[1,512]{1,0:T(1,128)}, f32[1,512]{1,0:T(1,128)}) custom-call(bf16[4,256,512]{2,1,0:T(8,128)(2,1)} %bitcast.6, bf16[4,256,512]{2,1,0:T(8,128)(2,1)} %bitcast.7, bf16[9,1024,512]{2,1,0:T(8,128)(2,1)} %bitcast.5, f32[1,512]{1,0:T(1,128)} %gain_ref.1, ...), custom_call_target="tpu_custom_call" | custom-call | tf_op jit(solution)/shard_map/pipeline/pallas_call | solution.py:450
  165.3 0.0 copy-start.1
  165.3 0.0 copy-start
  165.3 19.4 %weight_grad.1 = f32[9,1024,512]{2,1,0:T(8,128)} custom-call(f32[9,1024,512]{2,1,0:T(8,128)} %get-tuple-element.8.sum_ref, bf16[4,256,1024]{2,1,0:T(8,128)(2,1)} %get-tuple-element.9.h_ref, bf16[4,256,512]{2,1,0:T(8,128)(2,1)} %get-tuple-element.10.dy_ref), custom_call_target="tpu_custom_call" | custom-call | tf_op jit(solution)/shard_map/weight_grad/pallas_call | solution.py:498
  184.7 0.0 copy-done.1
  184.7 0.6 copy.10
  185.3 0.0 copy-done
  185.3 0.6 copy.11
Async XLA Ops:
  165.3 19.4 %copy-start.1 = (f32[1,512]{1,0:T(1,128)S(1)}, f32[1,512]{1,0:T(1,128)}, u32[]{:S(2)}) copy-start(f32[1,512]{1,0:T(1,128)} %get-tuple-element.17) | copy-start | bytes 6148
  165.3 20.0 %copy-start = (f32[1,512]{1,0:T(1,128)S(1)}, f32[1,512]{1,0:T(1,128)}, u32[]{:S(2)}) copy-start(f32[1,512]{1,0:T(1,128)} %get-tuple-element.18) | copy-start | bytes 6148
